TPU v7x, 256 devices: a whole 4x4x8 slice. The times are simulated.
256 devices in a mesh: leaf: 64 (over y, z, core), front: 4 (over x).
Axes of the slice: x: 4, y: 4, z: 8, core: 2. Of those that a mesh axis runs over, the one named last changes fastest.
Arguments:
- resid: float32 [262144, 128], P(('leaf', 'front')), may hold values from -6 to 6
- rec_owner: int32 [262144, 1], P(('leaf', 'front')), may hold values from 0 to 63; in each aligned block of 1024 rows (0 to 1023, 1024 to 2047, ...) at most 32 rows name the same one
- rec_cell: int32 [262144], P(('leaf', 'front')), may hold values from 0 to 511
- leaf_inverse: float32 [64, 2, 512, 512], P('leaf', None, 'front'), may hold values from -0.1875 to 0.1875
- couple_up: float32 [64, 3, 2, 1024, 512], P('leaf', None, None, None, 'front'), may hold values from -0.0625 to 0.0625
- sep_inverse: float32 [64, 2, 1024, 1024], P('leaf', None, 'front'), may hold values from -0.125 to 0.125
- couple_down: float32 [64, 3, 2, 512, 1024], P('leaf', None, None, 'front'), may hold values from -0.078125 to 0.078125
- forward_field: float32 [32768, 128], P(('leaf', 'front')), may hold values from -6 to 6
Outputs:
- gradient: float32 [32768], P(('leaf', 'front'))
Inputs may be any that keep to these rules, and one draw needn't show every extreme that they name: `rec_owner`: among the receivers of one device at most 32 lie in one subtree, and in every draw some subtree gets exactly 32 from some device.
All inputs are finite; a program needn't handle non-finite values.
Results may differ from a plain program's by a relative error of at most 0.0001.
Values sent between devices are 32-bit elements; how exact they have to be, the bound alone decides.
A program may use at most 64 MiB of HBM per device.

v0:
```python
import jax
import jax.numpy as jnp
from jax import lax
from jax.sharding import PartitionSpec as P


def from_partner(value, axis, stride):
    return lax.ppermute(value, axis, [(i, i ^ 1 << stride) for i in range(lax.axis_size(axis))])


def rotate(field):
    half = field.shape[-1] // 2
    return jnp.concatenate([-field[..., half:], field[..., :half]], -1)


def complex_apply(form, mats_real, mats_imag, field):
    first = jnp.einsum(form, mats_real, field, precision=lax.Precision.HIGHEST)
    second = jnp.einsum(form, mats_imag, field, precision=lax.Precision.HIGHEST)
    return first + rotate(second)


def gather_up(stack, levels):
    for level in range(levels):
        partner = from_partner(stack[level:], "leaf", level)
        stack = jnp.concatenate([stack[:level], stack[level:] + partner], 0)
    return stack


def local(
    resid, rec_owner, rec_cell, leaf_inverse, couple_up, sep_inverse, couple_down, forward_field
):
    leaf_count = lax.axis_size("leaf")
    row_count = resid.shape[0]
    columns = resid.shape[1]
    capacity = 2 * row_count // leaf_count
    owners = rec_owner[:, 0]
    member = (owners[:, None] == jnp.arange(leaf_count, dtype=jnp.int32)[None, :]).astype(jnp.int32)
    before = jnp.cumsum(member, 0) - member
    placed = owners * capacity + jnp.sum(before * member, 1)
    values = jnp.zeros((leaf_count * capacity, columns), jnp.float32).at[placed].set(resid)
    offsets = (
        jnp.full((leaf_count * capacity,), -1.0, jnp.float32)
        .at[placed]
        .set(rec_cell.astype(jnp.float32))
    )
    values, offsets = (
        lax.all_to_all(
            values.reshape(leaf_count, capacity, columns),
            "leaf",
            split_axis=0,
            concat_axis=0,
            tiled=True,
        ),
        lax.all_to_all(
            offsets.reshape(leaf_count, capacity), "leaf", split_axis=0, concat_axis=0, tiled=True
        ),
    )
    leaf_cells = leaf_inverse.shape[3]
    matches = (
        offsets.reshape(-1)[:, None] == jnp.arange(leaf_cells, dtype=jnp.float32)[None, :]
    ).astype(jnp.float32)
    partial_source = lax.dot_general(
        matches,
        values.reshape(-1, columns),
        (((0,), (0,)), ((), ())),
        precision=lax.Precision.HIGHEST,
    )
    source = lax.psum(partial_source, "front")
    forward_rows = complex_apply("ab,bc->ac", leaf_inverse[0, 0], leaf_inverse[0, 1], source)
    terms = -complex_apply("ksb,bc->ksc", couple_up[0, :, 0], couple_up[0, :, 1], forward_rows)
    levels = terms.shape[0]
    nextup = lax.axis_index("leaf") + 1
    owned = jnp.stack([nextup % 2 ** (level + 1) == 2**level for level in range(levels)]).astype(
        jnp.float32
    )
    summed = lax.psum(terms, "front")
    summed = gather_up(summed, levels)
    pending = jnp.sum(owned[:, None, None] * summed, 0)
    node_rows = complex_apply("ab,bc->ac", sep_inverse[0, 0], sep_inverse[0, 1], pending)
    ancestors = owned[:, None, None] * node_rows[None]
    for level in range(levels):
        partner = from_partner(ancestors[level:], "leaf", level)
        ancestors = jnp.concatenate([ancestors[:level], ancestors[level:] + partner], 0)
    block = couple_down[0]
    correction = complex_apply(
        "kab,kbc->ac",
        block[:, 0],
        block[:, 1],
        lax.all_gather(ancestors, "front", axis=1, tiled=True),
    )
    adjoint = forward_rows - correction
    half = columns // 2
    product = (
        forward_field[:, :half] * adjoint[:, :half] - forward_field[:, half:] * adjoint[:, half:]
    )
    return 0.125 * jnp.sum(product, 1)


def solution(mesh):
    placed = (
        P(("leaf", "front"), None),
        P(("leaf", "front"), None),
        P(("leaf", "front")),
        P("leaf", None, "front", None),
        P("leaf", None, None, None, "front"),
        P("leaf", None, "front", None),
        P("leaf", None, None, "front", None),
        P(("leaf", "front"), None),
    )
    return jax.shard_map(
        local, mesh=mesh, in_specs=placed, out_specs=P(("leaf", "front")), check_vma=False
    )
```

profile of v0, /device:TPU:1, one launch (start us, length us, event | category | flops | bytes accessed | tf_op | source)
XLA Modules:
  0.0 324.1 jit_solution(14532982105282108531)
XLA Ops:
  7.3 18.0 %reduce-window.6 = s32[64,8,128]{2,1,0:T(8,128)S(1)} reduce-window(s32[64,8,128]{2,1,0:T(8,128)S(1)} %fusion.39, s32[]{:T(128)} %constant.45.clone.1), window={size=1x1x128 pad=0_0x0_0x127_0}, to_apply=%region_0.0 | reduce-window | flops 8323072 | bytes 524292 | tf_op jit(solution)/shard_map/reduce-window
  26.0 4.3 %scatter_custom_fusion = f32[2048]{0:T(1024)S(1)} fusion(s32[1024]{0:T(1024)S(1)} %bitcast.119, f32[1024]{0:T(1024)S(1)} %convert_element_type.20, f32[]{:T(128)} %constant.43.clone.1), kind=kCustom, calls=%fused_computation.68 | custom fusion | bytes 8196 | tf_op jit(solution)/shard_map/scatter | solution.py:44
  31.0 13.2 %all-to-all-start = ((f32[64,1,32]{2,1,0:T(1,128)}), f32[64,1,32]{2,1,0:T(1,128)S(1)}, u32[]{:S(2)}, u32[]{:S(2)}) async-start(f32[64,1,32]{2,1,0:T(1,128)} %bitcast.6), calls=%async_computation | async-start | bytes 65536 | tf_op jit(solution)/shard_map/all_to_all | solution.py:54
  44.2 4.5 %scatter_custom_fusion.1 = f32[2048,128]{1,0:T(8,128)} fusion(s32[1024]{0:T(1024)S(1)} %bitcast.120, f32[1024,128]{1,0:T(8,128)} %param.8, f32[]{:T(128)} %constant.47.clone.1), kind=kCustom, calls=%fused_computation.39 | custom fusion | bytes 1049088 | tf_op jit(solution)/shard_map/scatter | solution.py:40
  48.7 4.8 %all-to-all-done = f32[64,1,32]{2,1,0:T(1,128)S(1)} async-done(((f32[64,1,32]{2,1,0:T(1,128)}), f32[64,1,32]{2,1,0:T(1,128)S(1)}, u32[]{:S(2)}, u32[]{:S(2)}) %all-to-all-start) | async-done | bytes 8224 | tf_op jit(solution)/shard_map/all_to_all | solution.py:54
  53.5 5.5 %all-to-all-start.1 = ((f32[64,32,128]{2,1,0:T(8,128)}), f32[64,32,128]{2,1,0:T(8,128)S(1)}, u32[]{:S(2)}, u32[]{:S(2)}) async-start(f32[64,32,128]{2,1,0:T(8,128)} %bitcast.7), calls=%async_computation.1 | async-start | bytes 2097152 | tf_op jit(solution)/shard_map/all_to_all | solution.py:47
  60.4 27.2 %all-to-all-done.1 = f32[64,32,128]{2,1,0:T(8,128)S(1)} async-done(((f32[64,32,128]{2,1,0:T(8,128)}), f32[64,32,128]{2,1,0:T(8,128)S(1)}, u32[]{:S(2)}, u32[]{:S(2)}) %all-to-all-start.1) | async-done | bytes 1048608 | tf_op jit(solution)/shard_map/all_to_all | solution.py:47
  88.5 5.8 %fusion = f32[512,128]{1,0:T(8,128)} fusion(f32[2048,128]{1,0:T(8,128)} %bitcast.113, f32[2048]{0:T(1024)S(1)} %eq.61), kind=kOutput, calls=%fused_computation.3 | convolution fusion | flops 1611661312 | bytes 1318912 | tf_op jit(solution)/shard_map/dot_general | solution.py:62
  94.6 41.4 %all-reduce.3.cloned.1.call-done = f32[512,128]{1,0:T(8,128)} async-done(((f32[512,128]{1,0:T(8,128)}), f32[512,128]{1,0:T(8,128)}) %all-reduce.3.cloned.1.call-update) | async-done | bytes 262160 | tf_op jit(solution)/shard_map/psum | solution.py:68
  136.0 1.6 convolution_bitcast_fusion.2
  140.8 2.7 fusion.7
  143.6 58.1 %all-reduce.5.cloned.1.call-done = f32[3,1024,128]{1,2,0:T(8,128)} async-done(((f32[3,1024,128]{1,2,0:T(8,128)}), f32[3,1024,128]{1,2,0:T(8,128)}) %all-reduce.5.cloned.1.call-update) | async-done | bytes 1572880 | tf_op jit(solution)/shard_map/psum | solution.py:76
  202.6 3.2 %collective-permute-done = f32[3,1024,128]{1,2,0:T(8,128)S(1)} collective-permute-done((f32[3,1024,128]{1,2,0:T(8,128)}, f32[3,1024,128]{1,2,0:T(8,128)S(1)}, u32[]{:S(2)}, u32[]{:S(2)}) %collective-permute-start) | collective-permute-done | bytes 1572896 | tf_op jit(solution)/shard_map/ppermute | solution.py:8
  205.9 1.7 add.64
  209.0 23.1 %collective-permute-done.1 = f32[2,1024,128]{1,2,0:T(8,128)S(1)} collective-permute-done((f32[2,1024,128]{1,2,0:T(8,128)S(1)}, f32[2,1024,128]{1,2,0:T(8,128)S(1)}, u32[]{:S(2)}, u32[]{:S(2)}) %collective-permute-start.1) | collective-permute-done | bytes 1048608 | tf_op jit(solution)/shard_map/ppermute | solution.py:8
  233.1 2.3 collective-permute-start.2
  235.5 22.8 %collective-permute-done.2 = f32[1,1024,128]{1,2,0:T(8,128)S(1)} collective-permute-done((f32[1,1024,128]{1,2,0:T(8,128)}, f32[1,1024,128]{1,2,0:T(8,128)S(1)}, u32[]{:S(2)}, u32[]{:S(2)}) %collective-permute-start.2) | collective-permute-done | bytes 524320 | tf_op jit(solution)/shard_map/ppermute | solution.py:8
  262.4 1.6 collective-permute-start.3
  266.1 7.1 %collective-permute-done.4 = f32[2,256,128]{1,2,0:T(8,128)S(1)} collective-permute-done((f32[2,256,128]{1,2,0:T(8,128)S(1)}, f32[2,256,128]{1,2,0:T(8,128)S(1)}, u32[]{:S(2)}, u32[]{:S(2)}) %collective-permute-start.4) | collective-permute-done | bytes 262176 | tf_op jit(solution)/shard_map/ppermute | solution.py:8
  273.2 2.6 collective-permute-start.5
  275.8 5.9 %collective-permute-done.5 = f32[1,256,128]{1,2,0:T(8,128)S(1)} collective-permute-done((f32[1,256,128]{1,2,0:T(8,128)S(1)}, f32[1,256,128]{1,2,0:T(8,128)S(1)}, u32[]{:S(2)}, u32[]{:S(2)}) %collective-permute-start.5) | collective-permute-done | bytes 131104 | tf_op jit(solution)/shard_map/ppermute | solution.py:8
  282.6 2.1 copy.36
  285.0 27.6 %all-gather.2.cloned.1.call-done = f32[3,1024,128]{1,2,0:T(8,128)} async-done(((f32[3,256,128]{1,2,0:T(8,128)}), f32[3,1024,128]{1,2,0:T(8,128)}) %all-gather.2.cloned.1.call-update) | async-done | bytes 1572880 | tf_op jit(solution)/shard_map/all_gather | solution.py:89
  312.6 2.9 fusion.21
  (70 shorter events, 20.5 us)
Async XLA Ops:
  6.5 19.3 %copy-start.6 = (s32[1024,1]{0,1:T(1,128)S(1)}, s32[1024,1]{0,1:T(1,128)}, u32[]{:S(2)}) copy-start(s32[1024,1]{0,1:T(1,128)} %param.9) | copy-start | bytes 12292
  6.5 19.4 %copy-start.7 = (s32[1024]{0:T(1024)S(1)}, s32[1024]{0:T(1024)}, u32[]{:S(2)}) copy-start(s32[1024]{0:T(1024)} %param.10) | copy-start | bytes 12292
  31.0 22.4 %all-to-all-start = ((f32[64,1,32]{2,1,0:T(1,128)}), f32[64,1,32]{2,1,0:T(1,128)S(1)}, u32[]{:S(2)}, u32[]{:S(2)}) async-start(f32[64,1,32]{2,1,0:T(1,128)} %bitcast.6), calls=%async_computation | async-start | bytes 65536 | tf_op jit(solution)/shard_map/all_to_all | solution.py:54
  53.5 34.1 %all-to-all-start.1 = ((f32[64,32,128]{2,1,0:T(8,128)}), f32[64,32,128]{2,1,0:T(8,128)S(1)}, u32[]{:S(2)}, u32[]{:S(2)}) async-start(f32[64,32,128]{2,1,0:T(8,128)} %bitcast.7), calls=%async_computation.1 | async-start | bytes 2097152 | tf_op jit(solution)/shard_map/all_to_all | solution.py:47
  59.0 77.0 %all-reduce.3.cloned.1.call-start = ((), (), s32[]{:S(2)}) async-start(), calls=%async_computation.2 | async-start | bytes 524288 | tf_op jit(solution)/shard_map/psum | solution.py:68
  87.5 1.0 copy-start.4
  88.5 50.7 %copy-start.2 = (f32[1,3,2,1024,128]{4,3,2,1,0:T(8,128)S(1)}, f32[1,3,2,1024,128]{4,3,2,1,0:T(8,128)}, u32[]{:S(2)}) copy-start(f32[1,3,2,1024,128]{4,3,2,1,0:T(8,128)} %param.12) | copy-start | bytes 9437188
  94.3 107.4 %all-reduce.5.cloned.1.call-start = ((), (), s32[]{:S(2)}) async-start(), calls=%async_computation.3 | async-start | bytes 3145728 | tf_op jit(solution)/shard_map/psum | solution.py:76
  143.6 169.0 %all-gather.2.cloned.1.call-start = ((), (), s32[]{:S(2)}) async-start(), calls=%async_computation.4 | async-start | bytes 1966080 | tf_op jit(solution)/shard_map/all_gather | solution.py:89
  201.8 4.1 %collective-permute-start = (f32[3,1024,128]{1,2,0:T(8,128)}, f32[3,1024,128]{1,2,0:T(8,128)S(1)}, u32[]{:S(2)}, u32[]{:S(2)}) collective-permute-start(f32[3,1024,128]{1,2,0:T(8,128)} %all-reduce.5.cloned.1.call-done), channel_id=1, source_target_pairs={{0,4},{4,0},{8,12},{12,8},{16,20},{20,16},{24,28},{28,24},{32,36},... | collective-permute-start | bytes 4718600 | tf_op jit(solution)/shard_map/ppermute | solution.py:8
  207.5 27.9 %copy-start = (f32[3,1024,128]{1,2,0:T(8,128)}, f32[3,1024,128]{1,2,0:T(8,128)S(1)}, u32[]{:S(2)}) copy-start(f32[3,1024,128]{1,2,0:T(8,128)S(1)} %add.64) | copy-start | bytes 4718596
  207.6 24.5 %collective-permute-start.1 = (f32[2,1024,128]{1,2,0:T(8,128)S(1)}, f32[2,1024,128]{1,2,0:T(8,128)S(1)}, u32[]{:S(2)}, u32[]{:S(2)}) collective-permute-start(f32[2,1024,128]{1,2,0:T(8,128)S(1)} %slice.131), channel_id=1, source_target_pairs={{0,8},{4,12},{8,0},{12,4},{16,24},{20,28},{24,16},{28,20},{32,40},... | collective-permute-start | bytes 3145736 | tf_op jit(solution)/shard_map/ppermute | solution.py:8
  233.1 25.1 %collective-permute-start.2 = (f32[1,1024,128]{1,2,0:T(8,128)}, f32[1,1024,128]{1,2,0:T(8,128)S(1)}, u32[]{:S(2)}, u32[]{:S(2)}) collective-permute-start(f32[1,1024,128]{1,2,0:T(8,128)} %slice.132), channel_id=1, source_target_pairs={{0,16},{4,20},{8,24},{12,28},{16,0},{20,4},{24,8},{28,12},{32,48},... | collective-permute-start | bytes 1572872 | tf_op jit(solution)/shard_map/ppermute | solution.py:8
  235.5 22.9 %slice-start = ((f32[3,1024,128]{1,2,0:T(8,128)}), f32[1,1024,128]{1,2,0:T(8,128)S(1)}, s32[]{:S(2)}) async-start(f32[3,1024,128]{1,2,0:T(8,128)} %copy-done), calls=%async_computation.5 | async-start | bytes 1048576 | tf_op jit(solution)/shard_map/slice | solution.py:25
  258.3 1.6 copy-start.3
  262.4 3.0 collective-permute-start.3
  265.5 7.6 %collective-permute-start.4 = (f32[2,256,128]{1,2,0:T(8,128)S(1)}, f32[2,256,128]{1,2,0:T(8,128)S(1)}, u32[]{:S(2)}, u32[]{:S(2)}) collective-permute-start(f32[2,256,128]{1,2,0:T(8,128)S(1)} %slice.136), channel_id=1, source_target_pairs={{0,8},{4,12},{8,0},{12,4},{16,24},{20,28},{24,16},{28,20},{32,40},... | collective-permute-start | bytes 786440 | tf_op jit(solution)/shard_map/ppermute | solution.py:8
  273.2 8.6 %collective-permute-start.5 = (f32[1,256,128]{1,2,0:T(8,128)S(1)}, f32[1,256,128]{1,2,0:T(8,128)S(1)}, u32[]{:S(2)}, u32[]{:S(2)}) collective-permute-start(f32[1,256,128]{1,2,0:T(8,128)S(1)} %slice.137), channel_id=1, source_target_pairs={{0,16},{4,20},{8,24},{12,28},{16,0},{20,4},{24,8},{28,12},{32,48},... | collective-permute-start | bytes 393224 | tf_op jit(solution)/shard_map/ppermute | solution.py:8
  282.6 2.2 copy-start.5
  312.6 3.0 copy-start.1
Sparse Core Ops, SparseCore 0:
  94.5 41.4 all-reduce.2
  143.7 58.0 all-reduce.4
  282.7 29.8 all-gather.1
where the time goes:
time: 325 us; the launch traced here: 324 us
  waiting for transfers between devices  223 us (69%)
  starting transfers between devices  28.2 us (9%)
  other arithmetic  23.7 us (7%)
  matrix products  20 us (6%)
  local copies, waits for them, and re-layouts  16.1 us (5%)
  between operations  13.4 us (4%)
    ppermute x6, waiting for transfers between devices, from_partner(): lax.ppermute(value, axis, [(i, i ^ 1 << stride) for i in range(lax.axis_s...  63.5 us
    psum x1, waiting for transfers between devices, local(): summed = lax.psum(terms, 'front')  58.1 us
    psum x1, waiting for transfers between devices, local(): source = lax.psum(partial_source, 'front')  41.4 us
    all_gather x1, waiting for transfers between devices, local(): lax.all_gather(ancestors, 'front', axis=1, tiled=True)  27.6 us
    all_to_all x1, waiting for transfers between devices, local(): lax.all_to_all(values.reshape(leaf_count, capacity, columns), 'leaf', spl...  27.2 us
    another operation x3, other arithmetic  18.2 us
    all_to_all x1, starting transfers between devices, local(): lax.all_to_all(offsets.reshape(leaf_count, capacity), 'leaf', split_axis=...  13.2 us
    ppermute x6, starting transfers between devices, from_partner(): lax.ppermute(value, axis, [(i, i ^ 1 << stride) for i in range(lax.axis_s...  9.23 us
  transfers between devices with their start and end apart: 11, of which 11 were waited for; matrix products, arithmetic and copies ran while one was open for 3% of the time, Pallas kernels for 0%

commit v1 on v0

v1 whole, which is shorter than its diff:
```python
import jax
import jax.numpy as jnp
from jax import lax
from jax.experimental import pallas as pl
from jax.experimental.pallas import tpu as pltpu
from jax.sharding import PartitionSpec as P

F32, BF16, I32 = jnp.float32, jnp.bfloat16, jnp.int32
MESH = pl.DeviceIdType.MESH
DMA = pltpu.SemaphoreType.DMA


def split(value):
    high = value.astype(BF16)
    return high, (value - high.astype(F32)).astype(BF16)


def dot(a, b):
    return jnp.dot(a, b, preferred_element_type=F32)


def rotate(field):
    lane = lax.broadcasted_iota(I32, field.shape, 1)
    turned = pltpu.roll(field, 64, 1)
    return jnp.where(lane < 64, -turned, turned)


def operand(field):
    high, low = split(field)
    turned_high, turned_low = split(rotate(field))
    return jnp.concatenate(
        [jnp.concatenate([high, low], 1), jnp.concatenate([turned_high, turned_low], 1)], 0
    )


def product(high, low, right):
    both = dot(high, right)
    return both[:, :128] + both[:, 128:] + dot(low, right[:, :128])


def wait_bytes(ref, sem):
    pltpu.make_async_copy(ref, ref, sem).wait()


def kernel(
    resid, owner, cell, leaf_inverse, couple_up, sep_inverse, couple_down, field, out,
    resid_v, rows_v, a_f, u_f, s_f, d_f, field_v,
    ah, al, uh, ul, sh, sl, dh, dl,
    send, recv, meta_send, meta_recv, part, part_recv, source,
    t_send, t_recv, t_sum, r1, r2, r3, s1, s2, s3, pend, sep, acc, fwd,
    load_sem, send_sem, recv_sem, meta_ssem, meta_rsem, x_ssem, x_rsem, g_ssem, g_rsem,
    core_ssem, core_rsem, rs_ssem, rs_rsem, p_ssem, p_rsem, z_ssem, b_ssem, f_ssem, b_rsem,
):
    leaf = lax.axis_index("leaf")
    x = lax.axis_index("front")
    c = lax.rem(leaf, 2)
    z = lax.rem(lax.div(leaf, 2), 8)
    y = lax.div(leaf, 16)
    zq, zl = lax.rem(z, 4), lax.rem(z, 2)
    base4, base8 = leaf - lax.rem(leaf, 4), leaf - lax.rem(leaf, 8)
    partner = leaf + 1 - 2 * c

    def remote(src, dst, ssem, rsem, to_leaf, to_front):
        return pltpu.make_async_remote_copy(
            src_ref=src, dst_ref=dst, send_sem=ssem, recv_sem=rsem,
            device_id=(to_leaf, to_front), device_id_type=MESH,
        )

    loads = [
        pltpu.make_async_copy(a, b, load_sem.at[i])
        for i, (a, b) in enumerate(
            [
                (resid, resid_v), (leaf_inverse, a_f), (couple_up, u_f),
                (sep_inverse, s_f), (couple_down, d_f), (field, field_v),
            ]
        )
    ]
    for load in loads:
        load.start()

    barrier = pltpu.get_barrier_semaphore()

    def greet(d, carry):
        pl.semaphore_signal(
            barrier, inc=1, device_id=(lax.rem(leaf + d, 64), x), device_id_type=MESH
        )
        return carry

    lax.fori_loop(1, 64, greet, 0)

    def greet_cube(k, carry):
        for dx in (1, 2, 3):
            pl.semaphore_signal(
                barrier, inc=1, device_id=(base8 + k, lax.rem(x + dx, 4)), device_id_type=MESH
            )
        return carry

    lax.fori_loop(0, 8, greet_cube, 0)

    leaf_ids = lax.broadcasted_iota(I32, (64, 128), 0)
    row_id = lax.broadcasted_iota(I32, (128, 128), 0)
    col_id = lax.broadcasted_iota(I32, (128, 128), 1)
    earlier = jnp.where(row_id < col_id, 1.0, 0.0).astype(BF16)
    lane_base = 32 * lax.rem(leaf, 4)
    count = jnp.zeros((64, 1), F32)
    meta = jnp.zeros((128, 128), F32)
    places = []
    for j in range(8):
        own = owner[j : j + 1, :]
        cells = cell[j : j + 1, :]
        member = jnp.where(own == leaf_ids, 1.0, 0.0)
        before = dot(member.astype(BF16), earlier) + count
        rank = jnp.sum(member * before, 0, keepdims=True).astype(I32)
        count = count + jnp.sum(member, 1, keepdims=True)
        places.append(own * 32 + rank)
        low = jnp.bitwise_and(cells, 31)
        parts = jnp.concatenate(
            [member * (cells - low).astype(F32), member * (low + 1).astype(F32)], 0
        ).astype(BF16)
        spot = jnp.where(rank == row_id - lane_base, 1.0, 0.0).astype(BF16)
        meta = meta + lax.dot_general(
            parts, spot, (((1,), (1,)), ((), ())), preferred_element_type=F32
        )
    meta_send[...] = (meta[:64] + meta[64:]).reshape(64, 1, 128)

    loads[0].wait()
    high, low = split(resid_v[...])
    rows_v[:, :128] = high
    rows_v[:, 128:] = low

    pl.semaphore_wait(barrier, 87)

    slot_ids = lax.broadcasted_iota(I32, (512, 128), 0)
    for dy in (2, 1, 3, 0):
        yd = lax.rem(y + dy, 4)
        slots = slot_ids + yd * 512
        pick = jnp.concatenate(
            [jnp.where(place == slots, 1.0, 0.0).astype(BF16) for place in places], 1
        )
        rows = dot(pick, rows_v[...])
        send[dy] = rows[:, :128] + rows[:, 128:]

        def push(k, carry):
            dz = lax.rem(lax.div(k, 2) * 3 + 4, 8)
            zd, cd = lax.rem(z + dz, 8), lax.rem(c + lax.rem(k, 2), 2)
            at = zd * 2 + cd
            to = yd * 16 + at
            src = send.at[dy, pl.ds(pl.multiple_of(at * 32, 32), 32)]
            dst = recv.at[pl.ds(pl.multiple_of(leaf * 32, 32), 32)]

            def far():
                remote(meta_send.at[to], meta_recv.at[leaf], meta_ssem, meta_rsem.at[y], to, x).start()
                remote(src, dst, send_sem, recv_sem.at[y], to, x).start()

            def near():
                pltpu.make_async_copy(meta_send.at[to], meta_recv.at[leaf], meta_rsem.at[y]).start()
                pltpu.make_async_copy(src, dst, recv_sem.at[y]).start()

            if dy:
                far()
            else:
                pl.when(to != leaf)(far)
                pl.when(to == leaf)(near)
            return carry

        lax.fori_loop(0, 16, push, 0)

    for load in loads[1:]:
        load.wait()
    for m in range(2):
        high, low = split(a_f[m])
        ah[:, m * 512 : m * 512 + 512] = high
        al[:, m * 512 : m * 512 + 512] = low

    def split_up(i, carry):
        level, at = lax.div(i, 8), pl.ds(pl.multiple_of(lax.rem(i, 8) * 128, 128), 128)
        for m in range(2):
            high, low = split(u_f[level, m, at])
            uh[level, at, m * 128 : m * 128 + 128] = high
            ul[level, at, m * 128 : m * 128 + 128] = low
        return carry

    lax.fori_loop(0, 24, split_up, 0)

    def split_sep(i, carry):
        at = pl.ds(pl.multiple_of(i * 32, 32), 32)
        for m in range(2):
            high, low = split(s_f[m, at])
            sh[at, m * 1024 : m * 1024 + 1024] = high
            sl[at, m * 1024 : m * 1024 + 1024] = low
        return carry

    lax.fori_loop(0, 8, split_sep, 0)

    def split_down(i, carry):
        level, at = lax.div(i, 4), pl.ds(pl.multiple_of(lax.rem(i, 4) * 32, 32), 32)
        for m in range(2):
            for f in range(4):
                high, low = split(d_f[level, m, at, f * 256 : f * 256 + 256])
                dh[level, f, at, m * 256 : m * 256 + 256] = high
                dl[level, f, at, m * 256 : m * 256 + 256] = low
        return carry

    lax.fori_loop(0, 12, split_down, 0)

    for step, dy in enumerate((2, 1, 3, 0)):
        ys = lax.rem(y + 4 - dy, 4)
        at = pl.ds(pl.multiple_of(ys * 512, 512), 512)
        wait_bytes(meta_recv.at[pl.ds(ys * 16, 16)], meta_rsem.at[ys])
        wait_bytes(recv.at[at], recv_sem.at[ys])
        hits = []
        for q in range(4):
            row = meta_recv[ys * 16 + q * 4]
            for i in range(1, 4):
                row = row + meta_recv[ys * 16 + q * 4 + i]
            hits.append(jnp.where(row.astype(I32) == slot_ids + 1, 1.0, 0.0).astype(BF16))
        both = dot(jnp.concatenate(hits, 1), jnp.concatenate(split(recv[at]), 1))
        both = both[:, :128] + both[:, 128:]
        if step:
            part[...] += both
        else:
            part[...] = both

    mine = pl.ds(pl.multiple_of(x * 128, 128), 128)
    scatter = [
        remote(
            part.at[pl.ds(pl.multiple_of(lax.rem(x + dx, 4) * 128, 128), 128)],
            part_recv.at[dx - 1], x_ssem.at[dx - 1], x_rsem.at[dx - 1], leaf, lax.rem(x + dx, 4),
        )
        for dx in (1, 2, 3)
    ]
    for copy in (scatter[1], scatter[0], scatter[2]):
        copy.start()
    for copy in scatter:
        copy.wait_recv()
    source[mine] = part[mine] + part_recv[0] + part_recv[1] + part_recv[2]
    gather = [
        remote(
            source.at[mine], source.at[mine], g_ssem.at[dx - 1], g_rsem.at[dx - 1],
            leaf, lax.rem(x + dx, 4),
        )
        for dx in (1, 2, 3)
    ]
    for copy in (gather[1], gather[0], gather[2]):
        copy.start()
    for copy in gather:
        copy.wait_recv()

    forward = product(ah[...], al[...], operand(source[...]))
    fwd[...] = forward
    right = operand(-forward)

    swaps = [
        remote(t_send.at[k], t_recv.at[k], core_ssem.at[k], core_rsem.at[k], partner, x)
        for k in range(3)
    ]
    theirs = pl.ds(pl.multiple_of((1 - c) * 512, 512), 512)
    ours = pl.ds(pl.multiple_of(c * 512, 512), 512)
    for k in (2, 1, 0):
        t_send[k] = product(uh[k, theirs], ul[k, theirs], right)
        swaps[k].start()
    for k in (2, 1, 0):
        t_sum[k] = product(uh[k, ours], ul[k, ours], right)

    stages = ((r1, s1, 1, 128, 0), (r2, s2, 2, 64, zl), (r3, s3, 4, 32, zq))
    for k in (2, 1, 0):
        box, _, span, rows, zk = stages[k]
        swaps[k].wait_recv()
        t_sum[k] += t_recv[k]
        me = zk * 4 + x
        box[me] = t_sum[k, pl.ds(pl.multiple_of(me * rows, rows), rows)]
        for dz in range(span):
            for dx in range(4):
                if dz or dx:
                    zt = lax.rem(zk + dz, span)
                    xt = lax.rem(x + dx, 4)
                    at = pl.ds(pl.multiple_of((zt * 4 + xt) * rows, rows), rows)
                    remote(
                        t_sum.at[k, at], box.at[me], rs_ssem.at[k], rs_rsem.at[k],
                        leaf + 2 * (zt - zk), xt,
                    ).start()

    targets = (leaf - c, base4 + 1, base8 + 3)
    for k in (2, 1, 0):
        box, total, span, rows, zk = stages[k]
        wait_bytes(box.at[pl.ds(0, 4 * span - 1)], rs_rsem.at[k])
        value = box[0]
        for i in range(1, 4 * span):
            value = value + box[i]
        total[...] = value
        at = pl.ds(pl.multiple_of(c * 512 + (zk * 4 + x) * rows, rows), rows)
        for f in range(4):
            local_one = jnp.logical_and(targets[k] == leaf, x == f)

            def far(k=k, f=f, total=total, at=at):
                remote(total, pend.at[at], p_ssem.at[k, f], p_rsem, targets[k], f).start()

            def near(k=k, f=f, total=total, at=at):
                pltpu.make_async_copy(total, pend.at[at], p_rsem).start()

            pl.when(jnp.logical_not(local_one))(far)
            pl.when(local_one)(near)

    owns = lax.rem(leaf, 8) != 7
    level_own = jnp.where(c == 0, 0, jnp.where(zl == 0, 1, 2))

    @pl.when(owns)
    def _():
        wait_bytes(pend, p_rsem)
        sep[level_own, x] = product(sh[...], sl[...], operand(pend[...]))

    def along_x(k):
        for dx in (2, 1, 3):
            xt = lax.rem(x + dx, 4)
            remote(sep.at[k, x], sep.at[k, x], b_ssem.at[k, dx - 1], b_rsem.at[k, x], leaf, xt).start()

    def across(k, f):
        remote(sep.at[k, f], sep.at[k, f], f_ssem.at[k, f], b_rsem.at[k, f], partner, x).start()

    def arrived(k, f):
        wait_bytes(sep.at[k, f], b_rsem.at[k, f])

    def along_z(k, i, to):
        return remote(sep.at[k, x], sep.at[k, x], z_ssem.at[i], b_rsem.at[k, x], to, x)

    z_sends2 = (along_z(1, 0, leaf + 2),)
    z_sends3 = (along_z(2, 0, base8 + 7), along_z(2, 1, base8 + 5), along_z(2, 2, base8 + 1))
    is2 = jnp.logical_and(c == 1, zl == 0)
    is3 = jnp.logical_and(c == 1, zq == 1)

    @pl.when(is2)
    def _():
        for copy in z_sends2:
            copy.start()

    @pl.when(is3)
    def _():
        for copy in z_sends3:
            copy.start()

    @pl.when(c == 0)
    def _():
        along_x(0)
        across(0, x)

    @pl.when(is2)
    def _():
        along_x(1)
        across(1, x)
        arrived(2, x)
        along_x(2)
        across(2, x)

    @pl.when(is3)
    def _():
        along_x(2)
        across(2, x)
        arrived(1, x)
        along_x(1)
        across(1, x)

    @pl.when(jnp.logical_and(c == 1, zq == 3))
    def _():
        for k in (1, 2):
            arrived(k, x)
            along_x(k)
            across(k, x)

    acc[...] = jnp.zeros_like(acc)

    def consume(f):
        for k in range(3):
            acc[...] += product(dh[k, f], dl[k, f], operand(sep[k, f]))

    @pl.when(c == 0)
    def _():
        for k in (1, 2):
            arrived(k, x)

    @pl.when(c == 1)
    def _():
        arrived(0, x)

    last = x
    for dx in (1, 3, 2):
        f = lax.rem(x + dx, 4)

        @pl.when(c == 0)
        def _():
            arrived(0, f)
            across(0, f)

        @pl.when(c == 1)
        def _():
            for k in (1, 2):
                arrived(k, f)
                across(k, f)

        consume(last)

        @pl.when(c == 0)
        def _():
            for k in (1, 2):
                arrived(k, f)

        @pl.when(c == 1)
        def _():
            arrived(0, f)

        last = f
    consume(last)

    weight = jnp.where(col_id < 64, 0.125, -0.125)
    value = field_v[...] * (fwd[...] - acc[...]) * weight
    out[...] = jnp.sum(value.T, 0, keepdims=True)

    wait_bytes(recv.at[pl.ds(0, 63 * 32)], send_sem)
    wait_bytes(meta_recv.at[pl.ds(0, 63)], meta_ssem)
    for copy in scatter + gather + swaps:
        copy.wait_send()
    for k in range(3):
        box, total, span, rows, zk = stages[k]
        wait_bytes(box.at[pl.ds(0, 4 * span - 1)], rs_ssem.at[k])
        for f in range(4):
            local_one = jnp.logical_and(targets[k] == leaf, x == f)

            @pl.when(jnp.logical_not(local_one))
            def _(k=k, f=f, total=total):
                wait_bytes(total, p_ssem.at[k, f])

    @pl.when(is2)
    def _():
        for copy in z_sends2:
            copy.wait_send()

    @pl.when(is3)
    def _():
        for copy in z_sends3:
            copy.wait_send()

    def drain(k):
        for dx in (1, 2, 3):
            wait_bytes(sep.at[k, x], b_ssem.at[k, dx - 1])
        for f in range(4):
            wait_bytes(sep.at[k, f], f_ssem.at[k, f])

    @pl.when(c == 0)
    def _():
        drain(0)

    @pl.when(c == 1)
    def _():
        drain(1)
        drain(2)


def local(
    resid, rec_owner, rec_cell, leaf_inverse, couple_up, sep_inverse, couple_down, forward_field
):
    vmem = pl.BlockSpec(memory_space=pltpu.VMEM)
    hbm = pl.BlockSpec(memory_space=pl.ANY)
    V = pltpu.VMEM
    out = pl.pallas_call(
        kernel,
        out_shape=jax.ShapeDtypeStruct((1, 128), F32),
        in_specs=[hbm, vmem, vmem, hbm, hbm, hbm, hbm, hbm],
        out_specs=vmem,
        scratch_shapes=[
            V((1024, 128), F32), V((1024, 256), BF16),
            V((2, 128, 512), F32), V((3, 2, 1024, 128), F32),
            V((2, 256, 1024), F32), V((3, 2, 128, 1024), F32), V((128, 128), F32),
            V((128, 1024), BF16), V((128, 1024), BF16),
            V((3, 1024, 256), BF16), V((3, 1024, 256), BF16),
            V((256, 2048), BF16), V((256, 2048), BF16),
            V((3, 4, 128, 512), BF16), V((3, 4, 128, 512), BF16),
            V((4, 512, 128), F32), V((2048, 128), F32),
            V((64, 1, 128), F32), V((64, 1, 128), F32),
            V((512, 128), F32), V((3, 128, 128), F32), V((512, 128), F32),
            V((3, 512, 128), F32), V((3, 512, 128), F32), V((3, 512, 128), F32),
            V((4, 128, 128), F32), V((8, 64, 128), F32), V((16, 32, 128), F32),
            V((128, 128), F32), V((64, 128), F32), V((32, 128), F32),
            V((1024, 128), F32), V((3, 4, 256, 128), F32), V((128, 128), F32), V((128, 128), F32),
            DMA((6,)), DMA, DMA((4,)), DMA, DMA((4,)), DMA((3,)), DMA((3,)), DMA((3,)), DMA((3,)),
            DMA((3,)), DMA((3,)), DMA((3,)), DMA((3,)), DMA((3, 4)), DMA,
            DMA((3,)), DMA((3, 3)), DMA((3, 4)), DMA((3, 4)),
        ],
        compiler_params=pltpu.CompilerParams(
            collective_id=0, has_side_effects=True, vmem_limit_bytes=48 * 1024 * 1024
        ),
        name="adjoint_gradient",
    )(
        resid, rec_owner.reshape(8, 128), rec_cell.reshape(8, 128), leaf_inverse[0], couple_up[0],
        sep_inverse[0], couple_down[0], forward_field,
    )
    return out.reshape(128)


def solution(mesh):
    placed = (
        P(("leaf", "front"), None),
        P(("leaf", "front"), None),
        P(("leaf", "front")),
        P("leaf", None, "front", None),
        P("leaf", None, None, None, "front"),
        P("leaf", None, "front", None),
        P("leaf", None, None, "front", None),
        P(("leaf", "front"), None),
    )
    return jax.shard_map(
        local, mesh=mesh, in_specs=placed, out_specs=P(("leaf", "front")), check_vma=False
    )
```

time: 325 us -> 89.1 us (0.27)
  waiting for transfers between devices: 223 us -> 0 us
  Pallas kernels: 0 us -> 82.4 us
  starting transfers between devices: 28.2 us -> 0 us
  other arithmetic: 23.7 us -> 0 us
  matrix products: 20 us -> 0 us
  between operations: 13.4 us -> 0.02 us
  local copies, waits for them, and re-layouts: 16.1 us -> 6.4 us
    psum x2 -> x0, waiting for transfers between devices: 99.5 us -> none  [the longest x1 58.1 us: local(): summed = lax.psum(terms, 'front')]
    pallas_call x0 -> x1, Pallas kernels: none -> 82.4 us  [local(): pl.pallas_call(kernel, out_shape=jax.ShapeDtypeStruct((1, 128), F32), in_...]
    ppermute x6 -> x0, waiting for transfers between devices: 63.5 us -> none  [from_partner(): lax.ppermute(value, axis, [(i, i ^ 1 << stride) for i in range(lax.axis_s...]
    all_to_all x2 -> x0, waiting for transfers between devices: 32 us -> none  [the longest x1 27.2 us: local(): lax.all_to_all(values.reshape(leaf_count, capacity, columns), 'leaf', spl...]
    all_gather x1 -> x0, waiting for transfers between devices: 27.6 us -> none  [local(): lax.all_gather(ancestors, 'front', axis=1, tiled=True)]
    dot_general x9 -> x0, matrix products: 20 us -> none  [the longest x4 7.22 us: complex_apply(): second = jnp.einsum(form, mats_imag, field, precision=lax.Precision.HIGHEST)]
    all_to_all x2 -> x0, starting transfers between devices: 18.7 us -> none  [the longest x1 13.2 us: local(): lax.all_to_all(offsets.reshape(leaf_count, capacity), 'leaf', split_axis=...]
    another operation x3 -> x0, other arithmetic: 18.2 us -> none
  transfers between devices with their start and end apart: 11 -> 0, of which waited for: 11 -> 0; matrix products, arithmetic and copies ran while one was open for 3% -> 0% of each run, Pallas kernels for 0% -> 0%
where the time goes in v1:
time: 89.1 us; the launch traced here: 88.8 us
  Pallas kernels  82.4 us (92%)
  local copies, waits for them, and re-layouts  6.4 us (7%)
    pallas_call x1, Pallas kernels, local(): pl.pallas_call(kernel, out_shape=jax.ShapeDtypeStruct((1, 128), F32), in_...  82.4 us
    unnamed x13, local copies, waits for them, and re-layouts  6.4 us

profile of v1, /device:TPU:1, one launch (start us, length us, event | category | flops | bytes accessed | tf_op | source)
XLA Modules:
  0.0 88.8 jit_solution(9994589783518306679)
XLA Ops:
  0.0 0.0 copy-start
  0.0 1.6 %copy-done = f32[1,2,256,1024]{3,2,1,0:T(8,128)S(1)} copy-done((f32[1,2,256,1024]{3,2,1,0:T(8,128)S(1)}, f32[1,2,256,1024]{3,2,1,0:T(8,128)}, u32[]{:S(2)}) %copy-start) | copy-done | bytes 2097176
  1.6 0.0 copy-start.1
  1.6 1.0 %copy-done.1 = f32[1024,128]{1,0:T(8,128)S(1)} copy-done((f32[1024,128]{1,0:T(8,128)S(1)}, f32[1024,128]{1,0:T(8,128)}, u32[]{:S(2)}) %copy-start.1) | copy-done | bytes 524312
  2.6 0.0 copy-start.2
  2.6 1.0 %copy-done.2 = f32[1,2,128,512]{3,2,1,0:T(8,128)S(1)} copy-done((f32[1,2,128,512]{3,2,1,0:T(8,128)S(1)}, f32[1,2,128,512]{3,2,1,0:T(8,128)}, u32[]{:S(2)}) %copy-start.2) | copy-done | bytes 524312
  3.7 0.0 copy-start.3
  3.7 0.8 copy-done.3
  4.5 0.0 copy-start.4
  4.5 0.7 copy-done.4
  5.2 0.0 copy-start.5
  5.2 0.7 copy-done.5
  5.9 82.4 %adjoint_gradient.1 = f32[1,128]{1,0:T(1,128)S(1)} custom-call(f32[1024,128]{1,0:T(8,128)S(1)} %copy-done.1, s32[8,128]{1,0:T(8,128)S(1)} %bitcast.9, s32[8,128]{1,0:T(8,128)S(1)} %bitcast.10, f32[2,128,512]{2,1,0:T(8,128)S(1)} %bitcast.8, f32[3,2,1024,128]{3,2,1,0:T(8,128)} %bitcast.12, f32[2,256,1024]{2,1,0:T(8,128)S(1)} %bitcast.7, ...), custom_call_target="tpu_custom_call" | custom-call | tf_op jit(solution)/shard_map/adjoint_gradient/pallas_call | solution.py:463
  88.3 0.5 copy.10
Async XLA Ops:
  0.0 1.6 %copy-start = (f32[1,2,256,1024]{3,2,1,0:T(8,128)S(1)}, f32[1,2,256,1024]{3,2,1,0:T(8,128)}, u32[]{:S(2)}) copy-start(f32[1,2,256,1024]{3,2,1,0:T(8,128)} %param.13) | copy-start | bytes 6291460
  1.6 1.0 %copy-start.1 = (f32[1024,128]{1,0:T(8,128)S(1)}, f32[1024,128]{1,0:T(8,128)}, u32[]{:S(2)}) copy-start(f32[1024,128]{1,0:T(8,128)} %resid.1) | copy-start | bytes 1572868
  2.6 1.0 %copy-start.2 = (f32[1,2,128,512]{3,2,1,0:T(8,128)S(1)}, f32[1,2,128,512]{3,2,1,0:T(8,128)}, u32[]{:S(2)}) copy-start(f32[1,2,128,512]{3,2,1,0:T(8,128)} %param.11) | copy-start | bytes 1572868
  3.7 0.8 copy-start.3
  4.5 0.7 copy-start.4
  5.2 0.7 copy-start.5

commit v2 on v1

--- a/solution.py
+++ b/solution.py
@@ -19,6 +19,10 @@
     return jnp.dot(a, b, preferred_element_type=F32)
 
 
+def dot_rows(a, b):
+    return lax.dot_general(a, b, (((1,), (1,)), ((), ())), preferred_element_type=F32)
+
+
 def rotate(field):
     lane = lax.broadcasted_iota(I32, field.shape, 1)
     turned = pltpu.roll(field, 64, 1)
@@ -43,12 +47,12 @@
 
 
 def kernel(
-    resid, owner, cell, leaf_inverse, couple_up, sep_inverse, couple_down, field, out,
-    resid_v, rows_v, a_f, u_f, s_f, d_f, field_v,
+    resid, owner_h, cell_h, leaf_inverse, couple_up, sep_inverse, couple_down, field, out,
+    owner, cell, resid_v, rows_v, a_f, u_f, s_f, d_f, field_v,
     ah, al, uh, ul, sh, sl, dh, dl,
-    send, recv, meta_send, meta_recv, part, part_recv, source,
+    send, recv, meta_send, meta_recv, part, z_recv, source,
     t_send, t_recv, t_sum, r1, r2, r3, s1, s2, s3, pend, sep, acc, fwd,
-    load_sem, send_sem, recv_sem, meta_ssem, meta_rsem, x_ssem, x_rsem, g_ssem, g_rsem,
+    load_sem, send_sem, recv_sem, meta_ssem, meta_rsem, zr_ssem, zr_rsem, g_ssem, g_rsem,
     core_ssem, core_rsem, rs_ssem, rs_rsem, p_ssem, p_rsem, z_ssem, b_ssem, f_ssem, b_rsem,
 ):
     leaf = lax.axis_index("leaf")
@@ -70,7 +74,7 @@
         pltpu.make_async_copy(a, b, load_sem.at[i])
         for i, (a, b) in enumerate(
             [
-                (resid, resid_v), (leaf_inverse, a_f), (couple_up, u_f),
+                (owner_h, owner), (cell_h, cell), (resid, resid_v), (leaf_inverse, a_f), (couple_up, u_f),
                 (sep_inverse, s_f), (couple_down, d_f), (field, field_v),
             ]
         )
@@ -80,30 +84,49 @@
 
     barrier = pltpu.get_barrier_semaphore()
 
-    def greet(d, carry):
-        pl.semaphore_signal(
-            barrier, inc=1, device_id=(lax.rem(leaf + d, 64), x), device_id_type=MESH
-        )
-        return carry
-
-    lax.fori_loop(1, 64, greet, 0)
-
-    def greet_cube(k, carry):
-        for dx in (1, 2, 3):
-            pl.semaphore_signal(
-                barrier, inc=1, device_id=(base8 + k, lax.rem(x + dx, 4)), device_id_type=MESH
-            )
-        return carry
-
-    lax.fori_loop(0, 8, greet_cube, 0)
-
+    def greet(to_leaf, to_front):
+        pl.semaphore_signal(barrier, inc=1, device_id=(to_leaf, to_front), device_id_type=MESH)
+
+    def greet_plane(dy, carry):
+        for cd in range(2):
+            for dx in (1, 2, 3):
+                greet((lax.rem(y + dy, 4) * 8 + z) * 2 + cd, lax.rem(x + dx, 4))
+        return carry
+
+    lax.fori_loop(0, 4, greet_plane, 0)
+
+    def greet_column(dy, carry):
+        for cd in range(2):
+            greet((lax.rem(y + dy, 4) * 8 + z) * 2 + cd, x)
+        return carry
+
+    lax.fori_loop(1, 4, greet_column, 0)
+    greet(partner, x)
+
+    def greet_z(dz, carry):
+        greet((y * 8 + lax.rem(z + dz, 8)) * 2 + c, x)
+        return carry
+
+    lax.fori_loop(1, 8, greet_z, 0)
+
+    def greet_cube(dz, carry):
+        at = base8 + 2 * lax.rem(zq + dz, 4)
+        greet(at + 1 - c, x)
+        for cd in range(2):
+            for dx in (1, 2, 3):
+                greet(at + cd, lax.rem(x + dx, 4))
+        return carry
+
+    lax.fori_loop(1, 4, greet_cube, 0)
+
+    loads[0].wait()
+    loads[1].wait()
     leaf_ids = lax.broadcasted_iota(I32, (64, 128), 0)
     row_id = lax.broadcasted_iota(I32, (128, 128), 0)
     col_id = lax.broadcasted_iota(I32, (128, 128), 1)
     earlier = jnp.where(row_id < col_id, 1.0, 0.0).astype(BF16)
-    lane_base = 32 * lax.rem(leaf, 4)
     count = jnp.zeros((64, 1), F32)
-    meta = jnp.zeros((128, 128), F32)
+    meta = jnp.zeros((32, 128), F32)
     places = []
     for j in range(8):
         own = owner[j : j + 1, :]
@@ -113,59 +136,74 @@
         rank = jnp.sum(member * before, 0, keepdims=True).astype(I32)
         count = count + jnp.sum(member, 1, keepdims=True)
         places.append(own * 32 + rank)
+        line = jnp.right_shift(own, 4) * 4 + jnp.bitwise_and(own, 1) * 2
+        line = line + jnp.bitwise_and(jnp.right_shift(own, 1), 1)
+        lane = jnp.bitwise_and(jnp.right_shift(own, 2), 3) * 32 + rank
+        on_line = jnp.where(line == leaf_ids[:16], 1.0, 0.0)
         low = jnp.bitwise_and(cells, 31)
         parts = jnp.concatenate(
-            [member * (cells - low).astype(F32), member * (low + 1).astype(F32)], 0
+            [on_line * (cells - low).astype(F32), on_line * (low + 1).astype(F32)], 0
         ).astype(BF16)
-        spot = jnp.where(rank == row_id - lane_base, 1.0, 0.0).astype(BF16)
-        meta = meta + lax.dot_general(
-            parts, spot, (((1,), (1,)), ((), ())), preferred_element_type=F32
-        )
-    meta_send[...] = (meta[:64] + meta[64:]).reshape(64, 1, 128)
-
-    loads[0].wait()
-    high, low = split(resid_v[...])
-    rows_v[:, :128] = high
-    rows_v[:, 128:] = low
-
-    pl.semaphore_wait(barrier, 87)
-
-    slot_ids = lax.broadcasted_iota(I32, (512, 128), 0)
-    for dy in (2, 1, 3, 0):
-        yd = lax.rem(y + dy, 4)
-        slots = slot_ids + yd * 512
-        pick = jnp.concatenate(
-            [jnp.where(place == slots, 1.0, 0.0).astype(BF16) for place in places], 1
-        )
-        rows = dot(pick, rows_v[...])
-        send[dy] = rows[:, :128] + rows[:, 128:]
-
-        def push(k, carry):
-            dz = lax.rem(lax.div(k, 2) * 3 + 4, 8)
-            zd, cd = lax.rem(z + dz, 8), lax.rem(c + lax.rem(k, 2), 2)
-            at = zd * 2 + cd
-            to = yd * 16 + at
-            src = send.at[dy, pl.ds(pl.multiple_of(at * 32, 32), 32)]
-            dst = recv.at[pl.ds(pl.multiple_of(leaf * 32, 32), 32)]
-
-            def far():
-                remote(meta_send.at[to], meta_recv.at[leaf], meta_ssem, meta_rsem.at[y], to, x).start()
-                remote(src, dst, send_sem, recv_sem.at[y], to, x).start()
-
-            def near():
-                pltpu.make_async_copy(meta_send.at[to], meta_recv.at[leaf], meta_rsem.at[y]).start()
-                pltpu.make_async_copy(src, dst, recv_sem.at[y]).start()
-
-            if dy:
-                far()
-            else:
-                pl.when(to != leaf)(far)
-                pl.when(to == leaf)(near)
-            return carry
-
-        lax.fori_loop(0, 16, push, 0)
-
-    for load in loads[1:]:
+        meta = meta + dot_rows(parts, jnp.where(lane == row_id, 1.0, 0.0).astype(BF16))
+    meta = meta[:16] + meta[16:]
+    for i in range(16):
+        meta_send[i // 2, i % 2 : i % 2 + 1, :] = meta[i : i + 1]
+
+    loads[2].wait()
+    high, low = split(resid_v[...].T)
+    rows_v[:128] = high
+    rows_v[128:] = low
+
+    pl.semaphore_wait(barrier, 59)
+
+    slot = lax.broadcasted_iota(I32, (256, 128), 0)
+    slot = (
+        jnp.bitwise_and(jnp.right_shift(slot, 7), 1) * 32
+        + jnp.bitwise_and(jnp.right_shift(slot, 5), 3) * 128
+        + jnp.bitwise_and(slot, 31)
+    )
+    me_plane = y * 8 + x * 2 + c
+    for h in range(2):
+        for dy in (2, 1, 3, 0):
+            yd = lax.rem(y + dy, 4)
+            slots = slot + (yd * 512 + h * 64)
+            pick = jnp.concatenate(
+                [jnp.where(place == slots, 1.0, 0.0).astype(BF16) for place in places], 1
+            )
+            rows = dot_rows(rows_v[...], pick)
+            rows = rows[:128] + rows[128:]
+            for cd in range(2):
+                send[h, dy, cd] = rows[:, cd * 128 : cd * 128 + 128]
+
+            def push(k, carry):
+                xt = lax.rem(x + 2 + lax.div(k, 2), 4)
+                cd = lax.rem(c + lax.rem(k, 2), 2)
+                to = (yd * 8 + z) * 2 + cd
+                src = send.at[h, dy, cd, pl.ds(pl.multiple_of(xt * 32, 32), 32)]
+                dst = recv.at[h, me_plane]
+                meta_src, meta_dst = meta_send.at[yd * 2 + cd], meta_recv.at[me_plane]
+
+                def far():
+                    if h == 0:
+                        remote(meta_src, meta_dst, meta_ssem, meta_rsem.at[y], to, xt).start()
+                    remote(src, dst, send_sem.at[h], recv_sem.at[h, y], to, xt).start()
+
+                def near():
+                    if h == 0:
+                        pltpu.make_async_copy(meta_src, meta_dst, meta_rsem.at[y]).start()
+                    pltpu.make_async_copy(src, dst, recv_sem.at[h, y]).start()
+
+                if dy:
+                    far()
+                else:
+                    self_copy = jnp.logical_and(to == leaf, xt == x)
+                    pl.when(jnp.logical_not(self_copy))(far)
+                    pl.when(self_copy)(near)
+                return carry
+
+            lax.fori_loop(0, 8, push, 0)
+
+    for load in loads[3:]:
         load.wait()
     for m in range(2):
         high, low = split(a_f[m])
@@ -203,37 +241,54 @@
 
     lax.fori_loop(0, 12, split_down, 0)
 
-    for step, dy in enumerate((2, 1, 3, 0)):
-        ys = lax.rem(y + 4 - dy, 4)
-        at = pl.ds(pl.multiple_of(ys * 512, 512), 512)
-        wait_bytes(meta_recv.at[pl.ds(ys * 16, 16)], meta_rsem.at[ys])
-        wait_bytes(recv.at[at], recv_sem.at[ys])
-        hits = []
-        for q in range(4):
-            row = meta_recv[ys * 16 + q * 4]
-            for i in range(1, 4):
-                row = row + meta_recv[ys * 16 + q * 4 + i]
-            hits.append(jnp.where(row.astype(I32) == slot_ids + 1, 1.0, 0.0).astype(BF16))
-        both = dot(jnp.concatenate(hits, 1), jnp.concatenate(split(recv[at]), 1))
-        both = both[:, :128] + both[:, 128:]
-        if step:
-            part[...] += both
-        else:
-            part[...] = both
-
-    mine = pl.ds(pl.multiple_of(x * 128, 128), 128)
-    scatter = [
-        remote(
-            part.at[pl.ds(pl.multiple_of(lax.rem(x + dx, 4) * 128, 128), 128)],
-            part_recv.at[dx - 1], x_ssem.at[dx - 1], x_rsem.at[dx - 1], leaf, lax.rem(x + dx, 4),
-        )
-        for dx in (1, 2, 3)
-    ]
-    for copy in (scatter[1], scatter[0], scatter[2]):
-        copy.start()
-    for copy in scatter:
-        copy.wait_recv()
-    source[mine] = part[mine] + part_recv[0] + part_recv[1] + part_recv[2]
+    cell_ids = lax.broadcasted_iota(I32, (512, 128), 0) + 1
+    diagonal = jnp.where(jnp.right_shift(row_id, 5) == jnp.right_shift(col_id, 5), 1.0, 0.0)
+    diagonal = diagonal.astype(BF16)
+    for h in range(2):
+        for step, dy in enumerate((2, 1, 3, 0)):
+            ys = lax.rem(y + 4 - dy, 4)
+            if h == 0:
+                wait_bytes(meta_recv.at[pl.ds(ys * 8, 8)], meta_rsem.at[ys])
+            wait_bytes(recv.at[h, pl.ds(ys * 8, 8)], recv_sem.at[h, ys])
+            hits, values = [], []
+            for i in range(8):
+                line = meta_recv[ys * 8 + i][h : h + 1, :].astype(I32)
+                hits.append(jnp.where(line == cell_ids, 1.0, 0.0).astype(BF16))
+                values.append(
+                    jnp.concatenate(
+                        [
+                            jnp.concatenate([piece] * 4, 0) * diagonal
+                            for piece in split(recv[h, ys * 8 + i])
+                        ],
+                        0,
+                    )
+                )
+            both = dot_rows(jnp.concatenate(values, 1), jnp.concatenate(hits, 1))
+            both = both[:128] + both[128:]
+            if step:
+                part[h] += both
+            else:
+                part[h] = both
+        for i in (2, 1, 3, 0):
+            zd = lax.rem(z + lax.rem(z + h, 2) + 2 * i, 8)
+            to = (y * 8 + zd) * 2 + c
+            src = part.at[h, pl.ds(pl.multiple_of(lax.div(zd, 2) * 32, 32), 32)]
+
+            def far(src=src, to=to):
+                remote(src, z_recv.at[z], zr_ssem, zr_rsem, to, x).start()
+
+            def near(src=src):
+                pltpu.make_async_copy(src, z_recv.at[z], zr_rsem).start()
+
+            pl.when(to != leaf)(far)
+            pl.when(to == leaf)(near)
+
+    mine = pl.ds(pl.multiple_of(x * 32, 32), 32)
+    wait_bytes(z_recv, zr_rsem)
+    total = z_recv[0]
+    for i in range(1, 8):
+        total = total + z_recv[i]
+    source[mine] = total
     gather = [
         remote(
             source.at[mine], source.at[mine], g_ssem.at[dx - 1], g_rsem.at[dx - 1],
@@ -246,7 +301,12 @@
     for copy in gather:
         copy.wait_recv()
 
-    forward = product(ah[...], al[...], operand(source[...]))
+    high, low = split(source[...])
+    right = jnp.concatenate(
+        [jnp.concatenate([p, jnp.concatenate([-p[64:], p[:64]], 0)], 1) for p in (high, low)], 0
+    )
+    both = dot_rows(ah[...], right)
+    forward = both[:, :128] + both[:, 128:] + dot_rows(al[...], right[:128])
     fwd[...] = forward
     right = operand(-forward)
 
@@ -414,9 +474,11 @@
     value = field_v[...] * (fwd[...] - acc[...]) * weight
     out[...] = jnp.sum(value.T, 0, keepdims=True)
 
-    wait_bytes(recv.at[pl.ds(0, 63 * 32)], send_sem)
-    wait_bytes(meta_recv.at[pl.ds(0, 63)], meta_ssem)
-    for copy in scatter + gather + swaps:
+    for h in range(2):
+        wait_bytes(recv.at[h, pl.ds(0, 31)], send_sem.at[h])
+    wait_bytes(meta_recv.at[pl.ds(0, 31)], meta_ssem)
+    wait_bytes(z_recv.at[pl.ds(0, 7)], zr_ssem)
+    for copy in gather + swaps:
         copy.wait_send()
     for k in range(3):
         box, total, span, rows, zk = stages[k]
@@ -463,29 +525,29 @@
     out = pl.pallas_call(
         kernel,
         out_shape=jax.ShapeDtypeStruct((1, 128), F32),
-        in_specs=[hbm, vmem, vmem, hbm, hbm, hbm, hbm, hbm],
+        in_specs=[hbm] * 8,
         out_specs=vmem,
         scratch_shapes=[
-            V((1024, 128), F32), V((1024, 256), BF16),
+            V((8, 128), I32), V((8, 128), I32), V((1024, 128), F32), V((256, 1024), BF16),
             V((2, 128, 512), F32), V((3, 2, 1024, 128), F32),
             V((2, 256, 1024), F32), V((3, 2, 128, 1024), F32), V((128, 128), F32),
             V((128, 1024), BF16), V((128, 1024), BF16),
             V((3, 1024, 256), BF16), V((3, 1024, 256), BF16),
             V((256, 2048), BF16), V((256, 2048), BF16),
             V((3, 4, 128, 512), BF16), V((3, 4, 128, 512), BF16),
-            V((4, 512, 128), F32), V((2048, 128), F32),
-            V((64, 1, 128), F32), V((64, 1, 128), F32),
-            V((512, 128), F32), V((3, 128, 128), F32), V((512, 128), F32),
+            V((2, 4, 2, 128, 128), F32), V((2, 32, 32, 128), F32),
+            V((8, 2, 128), F32), V((32, 2, 128), F32),
+            V((2, 128, 512), F32), V((8, 32, 512), F32), V((128, 512), F32),
             V((3, 512, 128), F32), V((3, 512, 128), F32), V((3, 512, 128), F32),
             V((4, 128, 128), F32), V((8, 64, 128), F32), V((16, 32, 128), F32),
             V((128, 128), F32), V((64, 128), F32), V((32, 128), F32),
             V((1024, 128), F32), V((3, 4, 256, 128), F32), V((128, 128), F32), V((128, 128), F32),
-            DMA((6,)), DMA, DMA((4,)), DMA, DMA((4,)), DMA((3,)), DMA((3,)), DMA((3,)), DMA((3,)),
+            DMA((8,)), DMA((2,)), DMA((2, 4)), DMA, DMA((4,)), DMA, DMA, DMA((3,)), DMA((3,)),
             DMA((3,)), DMA((3,)), DMA((3,)), DMA((3,)), DMA((3, 4)), DMA,
             DMA((3,)), DMA((3, 3)), DMA((3, 4)), DMA((3, 4)),
         ],
         compiler_params=pltpu.CompilerParams(
-            collective_id=0, has_side_effects=True, vmem_limit_bytes=48 * 1024 * 1024
+            collective_id=0, has_side_effects=True, vmem_limit_bytes=62 * 1024 * 1024
         ),
         name="adjoint_gradient",
     )(

time: 89.1 us -> 77.6 us (0.87)
  Pallas kernels: 82.4 us -> 76.3 us
  local copies, waits for them, and re-layouts: 6.4 us -> 1.19 us
    pallas_call x1, Pallas kernels: 82.4 us -> 76.3 us  [local(): pl.pallas_call(kernel, out_shape=jax.ShapeDtypeStruct((1, 128), F32), in_...]
    unnamed x13 -> x1, local copies, waits for them, and re-layouts: 6.4 us -> 1.19 us
where the time goes in v2:
time: 77.6 us; the launch traced here: 77.5 us
  Pallas kernels  76.3 us (98%)
  local copies, waits for them, and re-layouts  1.19 us (2%)
    pallas_call x1, Pallas kernels, local(): pl.pallas_call(kernel, out_shape=jax.ShapeDtypeStruct((1, 128), F32), in_...  76.3 us

profile of v2, /device:TPU:1, one launch (start us, length us, event | category | flops | bytes accessed | tf_op | source)
XLA Modules:
  0.0 77.5 jit_solution(14979132374812254229)
XLA Ops:
  0.0 76.3 %adjoint_gradient.1 = f32[1,128]{1,0:T(1,128)} custom-call(f32[1024,128]{1,0:T(8,128)} %resid.1, s32[8,128]{1,0:T(8,128)} %bitcast.11, s32[8,128]{1,0:T(8,128)} %bitcast.12, f32[2,128,512]{2,1,0:T(8,128)} %bitcast.10, f32[3,2,1024,128]{3,2,1,0:T(8,128)} %bitcast.7, f32[2,256,1024]{2,1,0:T(8,128)} %bitcast.9, f32[3,2,128,1024]{3,2,1,0:T(8,128)} %bitcast.8, ...), custom_call_target="tpu_custom_call" | custom-call | tf_op jit(solution)/shard_map/adjoint_gradient/pallas_call | solution.py:525
  76.3 1.2 %copy.10 = f32[128]{0:T(128)} copy(f32[128]{0:T(128)} %bitcast.13) | data formatting | bytes 1024

commit v3 on v2

--- a/solution.py
+++ b/solution.py
@@ -103,18 +103,28 @@
     lax.fori_loop(1, 4, greet_column, 0)
     greet(partner, x)
 
-    def greet_z(dz, carry):
-        greet((y * 8 + lax.rem(z + dz, 8)) * 2 + c, x)
-        return carry
-
-    lax.fori_loop(1, 8, greet_z, 0)
+    def greet_column_z(dz, carry):
+        greet((y * 8 + lax.rem(z + 2 * dz, 8)) * 2 + c, x)
+        return carry
+
+    lax.fori_loop(1, 4, greet_column_z, 0)
+
+    def greet_neighbour(k, carry):
+        for dx in range(4):
+            greet(lax.rem(k, 4) * 16 + lax.rem(z + 7 + 2 * c, 8) * 2 + lax.div(k, 4), lax.rem(x + dx, 4))
+        return carry
+
+    lax.fori_loop(0, 8, greet_neighbour, 0)
 
     def greet_cube(dz, carry):
         at = base8 + 2 * lax.rem(zq + dz, 4)
-        greet(at + 1 - c, x)
-        for cd in range(2):
-            for dx in (1, 2, 3):
-                greet(at + cd, lax.rem(x + dx, 4))
+        for dx in range(4):
+            greet(at + c, lax.rem(x + dx, 4))
+
+            @pl.when(jnp.logical_and(c == 1, jnp.logical_or(zq == 1, jnp.logical_and(zl == 0, dz == 1))))
+            def _():
+                greet(at, lax.rem(x + dx, 4))
+
         return carry
 
     lax.fori_loop(1, 4, greet_cube, 0)
@@ -147,14 +157,15 @@
         meta = meta + dot_rows(parts, jnp.where(lane == row_id, 1.0, 0.0).astype(BF16))
     meta = meta[:16] + meta[16:]
     for i in range(16):
-        meta_send[i // 2, i % 2 : i % 2 + 1, :] = meta[i : i + 1]
+        meta_send[i] = meta[i : i + 1]
 
     loads[2].wait()
     high, low = split(resid_v[...].T)
     rows_v[:128] = high
     rows_v[128:] = low
 
-    pl.semaphore_wait(barrier, 59)
+    greetings = 31 + 3 + 32 + 12 + (1 - c) * (4 * zl + jnp.where(zq == 1, 0, 4))
+    pl.semaphore_wait(barrier, greetings)
 
     slot = lax.broadcasted_iota(I32, (256, 128), 0)
     slot = (
@@ -163,10 +174,11 @@
         + jnp.bitwise_and(slot, 31)
     )
     me_plane = y * 8 + x * 2 + c
-    for h in range(2):
+    for h in (1, 0):
+        parity = lax.rem(z + h, 2)
         for dy in (2, 1, 3, 0):
             yd = lax.rem(y + dy, 4)
-            slots = slot + (yd * 512 + h * 64)
+            slots = slot + (yd * 512 + parity * 64)
             pick = jnp.concatenate(
                 [jnp.where(place == slots, 1.0, 0.0).astype(BF16) for place in places], 1
             )
@@ -178,22 +190,22 @@
             def push(k, carry):
                 xt = lax.rem(x + 2 + lax.div(k, 2), 4)
                 cd = lax.rem(c + lax.rem(k, 2), 2)
-                to = (yd * 8 + z) * 2 + cd
+                zt = lax.rem(z + 1 + 6 * cd, 8) if h else z
+                to = (yd * 8 + zt) * 2 + cd
                 src = send.at[h, dy, cd, pl.ds(pl.multiple_of(xt * 32, 32), 32)]
                 dst = recv.at[h, me_plane]
-                meta_src, meta_dst = meta_send.at[yd * 2 + cd], meta_recv.at[me_plane]
+                meta_src = meta_send.at[yd * 4 + cd * 2 + parity]
+                meta_dst = meta_recv.at[h, me_plane]
 
                 def far():
-                    if h == 0:
-                        remote(meta_src, meta_dst, meta_ssem, meta_rsem.at[y], to, xt).start()
+                    remote(meta_src, meta_dst, meta_ssem.at[h], meta_rsem.at[h, y], to, xt).start()
                     remote(src, dst, send_sem.at[h], recv_sem.at[h, y], to, xt).start()
 
                 def near():
-                    if h == 0:
-                        pltpu.make_async_copy(meta_src, meta_dst, meta_rsem.at[y]).start()
+                    pltpu.make_async_copy(meta_src, meta_dst, meta_rsem.at[h, y]).start()
                     pltpu.make_async_copy(src, dst, recv_sem.at[h, y]).start()
 
-                if dy:
+                if dy or h:
                     far()
                 else:
                     self_copy = jnp.logical_and(to == leaf, xt == x)
@@ -244,15 +256,14 @@
     cell_ids = lax.broadcasted_iota(I32, (512, 128), 0) + 1
     diagonal = jnp.where(jnp.right_shift(row_id, 5) == jnp.right_shift(col_id, 5), 1.0, 0.0)
     diagonal = diagonal.astype(BF16)
-    for h in range(2):
-        for step, dy in enumerate((2, 1, 3, 0)):
+    for h in (1, 0):
+        for dy in (2, 1, 3, 0):
             ys = lax.rem(y + 4 - dy, 4)
-            if h == 0:
-                wait_bytes(meta_recv.at[pl.ds(ys * 8, 8)], meta_rsem.at[ys])
+            wait_bytes(meta_recv.at[h, pl.ds(ys * 8, 8)], meta_rsem.at[h, ys])
             wait_bytes(recv.at[h, pl.ds(ys * 8, 8)], recv_sem.at[h, ys])
             hits, values = [], []
             for i in range(8):
-                line = meta_recv[ys * 8 + i][h : h + 1, :].astype(I32)
+                line = meta_recv[h, ys * 8 + i].astype(I32)
                 hits.append(jnp.where(line == cell_ids, 1.0, 0.0).astype(BF16))
                 values.append(
                     jnp.concatenate(
@@ -265,28 +276,24 @@
                 )
             both = dot_rows(jnp.concatenate(values, 1), jnp.concatenate(hits, 1))
             both = both[:128] + both[128:]
-            if step:
-                part[h] += both
+            if h and dy == 2:
+                part[...] = both
             else:
-                part[h] = both
-        for i in (2, 1, 3, 0):
-            zd = lax.rem(z + lax.rem(z + h, 2) + 2 * i, 8)
-            to = (y * 8 + zd) * 2 + c
-            src = part.at[h, pl.ds(pl.multiple_of(lax.div(zd, 2) * 32, 32), 32)]
-
-            def far(src=src, to=to):
-                remote(src, z_recv.at[z], zr_ssem, zr_rsem, to, x).start()
-
-            def near(src=src):
-                pltpu.make_async_copy(src, z_recv.at[z], zr_rsem).start()
-
-            pl.when(to != leaf)(far)
-            pl.when(to == leaf)(near)
+                part[...] += both
+
+    zh = lax.div(z, 2)
+    for i in (2, 1, 3, 0):
+        zd = lax.rem(z + 2 * i, 8)
+        src = part.at[pl.ds(pl.multiple_of(lax.div(zd, 2) * 32, 32), 32)]
+        if i:
+            remote(src, z_recv.at[zh], zr_ssem, zr_rsem, (y * 8 + zd) * 2 + c, x).start()
+        else:
+            pltpu.make_async_copy(src, z_recv.at[zh], zr_rsem).start()
 
     mine = pl.ds(pl.multiple_of(x * 32, 32), 32)
     wait_bytes(z_recv, zr_rsem)
     total = z_recv[0]
-    for i in range(1, 8):
+    for i in range(1, 4):
         total = total + z_recv[i]
     source[mine] = total
     gather = [
@@ -475,9 +482,9 @@
     out[...] = jnp.sum(value.T, 0, keepdims=True)
 
     for h in range(2):
-        wait_bytes(recv.at[h, pl.ds(0, 31)], send_sem.at[h])
-    wait_bytes(meta_recv.at[pl.ds(0, 31)], meta_ssem)
-    wait_bytes(z_recv.at[pl.ds(0, 7)], zr_ssem)
+        wait_bytes(recv.at[h, pl.ds(0, 31 + h)], send_sem.at[h])
+        wait_bytes(meta_recv.at[h, pl.ds(0, 31 + h)], meta_ssem.at[h])
+    wait_bytes(z_recv.at[pl.ds(0, 3)], zr_ssem)
     for copy in gather + swaps:
         copy.wait_send()
     for k in range(3):
@@ -536,13 +543,13 @@
             V((256, 2048), BF16), V((256, 2048), BF16),
             V((3, 4, 128, 512), BF16), V((3, 4, 128, 512), BF16),
             V((2, 4, 2, 128, 128), F32), V((2, 32, 32, 128), F32),
-            V((8, 2, 128), F32), V((32, 2, 128), F32),
-            V((2, 128, 512), F32), V((8, 32, 512), F32), V((128, 512), F32),
+            V((16, 1, 128), F32), V((2, 32, 1, 128), F32),
+            V((128, 512), F32), V((4, 32, 512), F32), V((128, 512), F32),
             V((3, 512, 128), F32), V((3, 512, 128), F32), V((3, 512, 128), F32),
             V((4, 128, 128), F32), V((8, 64, 128), F32), V((16, 32, 128), F32),
             V((128, 128), F32), V((64, 128), F32), V((32, 128), F32),
             V((1024, 128), F32), V((3, 4, 256, 128), F32), V((128, 128), F32), V((128, 128), F32),
-            DMA((8,)), DMA((2,)), DMA((2, 4)), DMA, DMA((4,)), DMA, DMA, DMA((3,)), DMA((3,)),
+            DMA((8,)), DMA((2,)), DMA((2, 4)), DMA((2,)), DMA((2, 4)), DMA, DMA, DMA((3,)), DMA((3,)),
             DMA((3,)), DMA((3,)), DMA((3,)), DMA((3,)), DMA((3, 4)), DMA,
             DMA((3,)), DMA((3, 3)), DMA((3, 4)), DMA((3, 4)),
         ],

time: 77.6 us -> 76.1 us (0.981)
  Pallas kernels: 76.3 us -> 74.8 us
    pallas_call x1, Pallas kernels: 76.3 us -> 74.8 us  [local(): pl.pallas_call(kernel, out_shape=jax.ShapeDtypeStruct((1, 128), F32), in_...]
where the time goes in v3:
time: 76.1 us; the launch traced here: 76 us
  Pallas kernels  74.8 us (98%)
  local copies, waits for them, and re-layouts  1.19 us (2%)
    pallas_call x1, Pallas kernels, local(): pl.pallas_call(kernel, out_shape=jax.ShapeDtypeStruct((1, 128), F32), in_...  74.8 us

profile of v3, /device:TPU:1, one launch (start us, length us, event | category | flops | bytes accessed | tf_op | source)
XLA Modules:
  0.0 76.0 jit_solution(10196786814362320717)
XLA Ops:
  0.0 74.8 %adjoint_gradient.1 = f32[1,128]{1,0:T(1,128)} custom-call(f32[1024,128]{1,0:T(8,128)} %resid.1, s32[8,128]{1,0:T(8,128)} %bitcast.11, s32[8,128]{1,0:T(8,128)} %bitcast.12, f32[2,128,512]{2,1,0:T(8,128)} %bitcast.10, f32[3,2,1024,128]{3,2,1,0:T(8,128)} %bitcast.7, f32[2,256,1024]{2,1,0:T(8,128)} %bitcast.9, f32[3,2,128,1024]{3,2,1,0:T(8,128)} %bitcast.8, ...), custom_call_target="tpu_custom_call" | custom-call | tf_op jit(solution)/shard_map/adjoint_gradient/pallas_call | solution.py:532
  74.8 1.2 %copy.10 = f32[128]{0:T(128)} copy(f32[128]{0:T(128)} %bitcast.13) | data formatting | bytes 1024

commit v4 on v3

--- a/solution.py
+++ b/solution.py
@@ -37,9 +37,10 @@
     )
 
 
-def product(high, low, right):
-    both = dot(high, right)
-    return both[:, :128] + both[:, 128:] + dot(low, right[:, :128])
+def folded(both):
+    half = both.shape[0] // 2
+    both = both[:, :128] + both[:, 128:]
+    return both[:half] + both[half:]
 
 
 def wait_bytes(ref, sem):
@@ -49,11 +50,11 @@
 def kernel(
     resid, owner_h, cell_h, leaf_inverse, couple_up, sep_inverse, couple_down, field, out,
     owner, cell, resid_v, rows_v, a_f, u_f, s_f, d_f, field_v,
-    ah, al, uh, ul, sh, sl, dh, dl,
+    ap, uh, ul, sp, dp,
     send, recv, meta_send, meta_recv, part, z_recv, source,
     t_send, t_recv, t_sum, r1, r2, r3, s1, s2, s3, pend, sep, acc, fwd,
     load_sem, send_sem, recv_sem, meta_ssem, meta_rsem, zr_ssem, zr_rsem, g_ssem, g_rsem,
-    core_ssem, core_rsem, rs_ssem, rs_rsem, p_ssem, p_rsem, z_ssem, b_ssem, f_ssem, b_rsem,
+    core_ssem, core_rsem, rs_ssem, rs_rsem, p_ssem, p_rsem, z_ssem, b_ssem, h_ssem, f_ssem, b_rsem,
 ):
     leaf = lax.axis_index("leaf")
     x = lax.axis_index("front")
@@ -219,8 +220,8 @@
         load.wait()
     for m in range(2):
         high, low = split(a_f[m])
-        ah[:, m * 512 : m * 512 + 512] = high
-        al[:, m * 512 : m * 512 + 512] = low
+        ap[:128, m * 512 : m * 512 + 512] = high
+        ap[128:, m * 512 : m * 512 + 512] = low
 
     def split_up(i, carry):
         level, at = lax.div(i, 8), pl.ds(pl.multiple_of(lax.rem(i, 8) * 128, 128), 128)
@@ -233,22 +234,23 @@
     lax.fori_loop(0, 24, split_up, 0)
 
     def split_sep(i, carry):
-        at = pl.ds(pl.multiple_of(i * 32, 32), 32)
+        start = pl.multiple_of(i * 32, 32)
         for m in range(2):
-            high, low = split(s_f[m, at])
-            sh[at, m * 1024 : m * 1024 + 1024] = high
-            sl[at, m * 1024 : m * 1024 + 1024] = low
+            for q in range(4):
+                high, low = split(s_f[m, pl.ds(start, 32), q * 256 : q * 256 + 256])
+                sp[q, pl.ds(start, 32), m * 256 : m * 256 + 256] = high
+                sp[q, pl.ds(start + 256, 32), m * 256 : m * 256 + 256] = low
         return carry
 
     lax.fori_loop(0, 8, split_sep, 0)
 
     def split_down(i, carry):
-        level, at = lax.div(i, 4), pl.ds(pl.multiple_of(lax.rem(i, 4) * 32, 32), 32)
+        level, start = lax.div(i, 4), pl.multiple_of(lax.rem(i, 4) * 32, 32)
         for m in range(2):
             for f in range(4):
-                high, low = split(d_f[level, m, at, f * 256 : f * 256 + 256])
-                dh[level, f, at, m * 256 : m * 256 + 256] = high
-                dl[level, f, at, m * 256 : m * 256 + 256] = low
+                high, low = split(d_f[level, m, pl.ds(start, 32), f * 256 : f * 256 + 256])
+                dp[level, f, pl.ds(start, 32), m * 256 : m * 256 + 256] = high
+                dp[level, f, pl.ds(start + 128, 32), m * 256 : m * 256 + 256] = low
         return carry
 
     lax.fori_loop(0, 12, split_down, 0)
@@ -282,29 +284,32 @@
                 part[...] += both
 
     zh = lax.div(z, 2)
-    for i in (2, 1, 3, 0):
-        zd = lax.rem(z + 2 * i, 8)
-        src = part.at[pl.ds(pl.multiple_of(lax.div(zd, 2) * 32, 32), 32)]
-        if i:
-            remote(src, z_recv.at[zh], zr_ssem, zr_rsem, (y * 8 + zd) * 2 + c, x).start()
-        else:
-            pltpu.make_async_copy(src, z_recv.at[zh], zr_rsem).start()
-
-    mine = pl.ds(pl.multiple_of(x * 32, 32), 32)
-    wait_bytes(z_recv, zr_rsem)
-    total = z_recv[0]
-    for i in range(1, 4):
-        total = total + z_recv[i]
-    source[mine] = total
-    gather = [
-        remote(
-            source.at[mine], source.at[mine], g_ssem.at[dx - 1], g_rsem.at[dx - 1],
-            leaf, lax.rem(x + dx, 4),
-        )
-        for dx in (1, 2, 3)
-    ]
-    for copy in (gather[1], gather[0], gather[2]):
-        copy.start()
+    for half in range(2):
+        for i in (2, 1, 3, 0):
+            zd = lax.rem(z + 2 * i, 8)
+            at = pl.multiple_of(lax.div(zd, 2) * 32 + half * 16, 16)
+            src, dst = part.at[pl.ds(at, 16)], z_recv.at[half, zh]
+            if i:
+                to = (y * 8 + zd) * 2 + c
+                remote(src, dst, zr_ssem.at[half], zr_rsem.at[half], to, x).start()
+            else:
+                pltpu.make_async_copy(src, dst, zr_rsem.at[half]).start()
+
+    gather = []
+    for half in range(2):
+        mine = pl.ds(pl.multiple_of(x * 32 + half * 16, 16), 16)
+        wait_bytes(z_recv.at[half], zr_rsem.at[half])
+        total = z_recv[half, 0]
+        for i in range(1, 4):
+            total = total + z_recv[half, i]
+        source[mine] = total
+        for dx in (2, 1, 3):
+            copy = remote(
+                source.at[mine], source.at[mine], g_ssem.at[half, dx - 1], g_rsem.at[half, dx - 1],
+                leaf, lax.rem(x + dx, 4),
+            )
+            copy.start()
+            gather.append(copy)
     for copy in gather:
         copy.wait_recv()
 
@@ -312,8 +317,7 @@
     right = jnp.concatenate(
         [jnp.concatenate([p, jnp.concatenate([-p[64:], p[:64]], 0)], 1) for p in (high, low)], 0
     )
-    both = dot_rows(ah[...], right)
-    forward = both[:, :128] + both[:, 128:] + dot_rows(al[...], right[:128])
+    forward = folded(dot_rows(ap[...], right))
     fwd[...] = forward
     right = operand(-forward)
 
@@ -323,21 +327,23 @@
     ]
     theirs = pl.ds(pl.multiple_of((1 - c) * 512, 512), 512)
     ours = pl.ds(pl.multiple_of(c * 512, 512), 512)
-    for k in (2, 1, 0):
-        t_send[k] = product(uh[k, theirs], ul[k, theirs], right)
+    stages = ((r1, s1, 1, 128, 0), (r2, s2, 2, 64, zl), (r3, s3, 4, 32, zq))
+
+    def term(k, at):
+        both = dot(uh[k, at], right)
+        return both[:, :128] + both[:, 128:] + dot(ul[k, at], right[:, :128])
+
+    def give(k):
+        t_send[k] = term(k, theirs)
         swaps[k].start()
-    for k in (2, 1, 0):
-        t_sum[k] = product(uh[k, ours], ul[k, ours], right)
-
-    stages = ((r1, s1, 1, 128, 0), (r2, s2, 2, 64, zl), (r3, s3, 4, 32, zq))
-    for k in (2, 1, 0):
+
+    def scatter(k):
         box, _, span, rows, zk = stages[k]
         swaps[k].wait_recv()
         t_sum[k] += t_recv[k]
         me = zk * 4 + x
-        box[me] = t_sum[k, pl.ds(pl.multiple_of(me * rows, rows), rows)]
         for dz in range(span):
-            for dx in range(4):
+            for dx in (2, 1, 3, 0):
                 if dz or dx:
                     zt = lax.rem(zk + dz, span)
                     xt = lax.rem(x + dx, 4)
@@ -346,9 +352,20 @@
                         t_sum.at[k, at], box.at[me], rs_ssem.at[k], rs_rsem.at[k],
                         leaf + 2 * (zt - zk), xt,
                     ).start()
+        box[me] = t_sum[k, pl.ds(pl.multiple_of(me * rows, rows), rows)]
+
+    give(0)
+    t_sum[0] = term(0, ours)
+    give(2)
+    scatter(0)
+    t_sum[2] = term(2, ours)
+    give(1)
+    scatter(2)
+    t_sum[1] = term(1, ours)
+    scatter(1)
 
     targets = (leaf - c, base4 + 1, base8 + 3)
-    for k in (2, 1, 0):
+    for k in (0, 2, 1):
         box, total, span, rows, zk = stages[k]
         wait_bytes(box.at[pl.ds(0, 4 * span - 1)], rs_rsem.at[k])
         value = box[0]
@@ -356,14 +373,15 @@
             value = value + box[i]
         total[...] = value
         at = pl.ds(pl.multiple_of(c * 512 + (zk * 4 + x) * rows, rows), rows)
+        quarter = c * 2 + lax.div(zk * 4 + x, 2 * span)
         for f in range(4):
             local_one = jnp.logical_and(targets[k] == leaf, x == f)
 
-            def far(k=k, f=f, total=total, at=at):
-                remote(total, pend.at[at], p_ssem.at[k, f], p_rsem, targets[k], f).start()
-
-            def near(k=k, f=f, total=total, at=at):
-                pltpu.make_async_copy(total, pend.at[at], p_rsem).start()
+            def far(k=k, f=f, total=total, at=at, quarter=quarter):
+                remote(total, pend.at[at], p_ssem.at[k, f], p_rsem.at[quarter], targets[k], f).start()
+
+            def near(k=k, f=f, total=total, at=at, quarter=quarter):
+                pltpu.make_async_copy(total, pend.at[at], p_rsem.at[quarter]).start()
 
             pl.when(jnp.logical_not(local_one))(far)
             pl.when(local_one)(near)
@@ -373,13 +391,26 @@
 
     @pl.when(owns)
     def _():
-        wait_bytes(pend, p_rsem)
-        sep[level_own, x] = product(sh[...], sl[...], operand(pend[...]))
+        both = None
+        for q in range(4):
+            at = pl.ds(q * 256, 256)
+            wait_bytes(pend.at[at], p_rsem.at[q])
+            more = dot(sp[q], operand(pend[at]))
+            both = more if both is None else both + more
+        sep[level_own, x] = folded(both)
 
     def along_x(k):
-        for dx in (2, 1, 3):
+        for dx in (1, 3):
             xt = lax.rem(x + dx, 4)
             remote(sep.at[k, x], sep.at[k, x], b_ssem.at[k, dx - 1], b_rsem.at[k, x], leaf, xt).start()
+
+    def relay(k, f, dx):
+        if dx != 2:
+            part_ref = sep.at[k, f, pl.ds(0 if dx == 1 else 128, 128)]
+            remote(
+                part_ref, part_ref, h_ssem.at[k, dx // 2], b_rsem.at[k, f],
+                leaf, lax.rem(x + 4 - dx, 4),
+            ).start()
 
     def across(k, f):
         remote(sep.at[k, f], sep.at[k, f], f_ssem.at[k, f], b_rsem.at[k, f], partner, x).start()
@@ -437,33 +468,34 @@
 
     def consume(f):
         for k in range(3):
-            acc[...] += product(dh[k, f], dl[k, f], operand(sep[k, f]))
-
-    @pl.when(c == 0)
-    def _():
-        for k in (1, 2):
-            arrived(k, x)
-
-    @pl.when(c == 1)
-    def _():
-        arrived(0, x)
-
-    last = x
-    for dx in (1, 3, 2):
+            acc[...] += folded(dot(dp[k, f], operand(sep[k, f])))
+
+    def take(k, dx):
         f = lax.rem(x + dx, 4)
-
+        arrived(k, f)
+        relay(k, f, dx)
+        across(k, f)
+
+    def take_all(steps):
         @pl.when(c == 0)
         def _():
-            arrived(0, f)
-            across(0, f)
-
-        @pl.when(c == 1)
+            for dx in steps:
+                take(0, dx)
+
+        @pl.when(is3)
+        def _():
+            for k in (2, 1):
+                for dx in steps:
+                    take(k, dx)
+
+        @pl.when(jnp.logical_and(c == 1, zq != 1))
         def _():
             for k in (1, 2):
-                arrived(k, f)
-                across(k, f)
-
-        consume(last)
+                for dx in steps:
+                    take(k, dx)
+
+    def use(dx):
+        f = lax.rem(x + dx, 4)
 
         @pl.when(c == 0)
         def _():
@@ -474,8 +506,14 @@
         def _():
             arrived(0, f)
 
-        last = f
-    consume(last)
+        consume(f)
+
+    take_all((1, 3))
+    use(0)
+    use(1)
+    use(3)
+    take_all((2,))
+    use(2)
 
     weight = jnp.where(col_id < 64, 0.125, -0.125)
     value = field_v[...] * (fwd[...] - acc[...]) * weight
@@ -484,7 +522,8 @@
     for h in range(2):
         wait_bytes(recv.at[h, pl.ds(0, 31 + h)], send_sem.at[h])
         wait_bytes(meta_recv.at[h, pl.ds(0, 31 + h)], meta_ssem.at[h])
-    wait_bytes(z_recv.at[pl.ds(0, 3)], zr_ssem)
+    for half in range(2):
+        wait_bytes(z_recv.at[half, pl.ds(0, 3)], zr_ssem.at[half])
     for copy in gather + swaps:
         copy.wait_send()
     for k in range(3):
@@ -508,8 +547,9 @@
             copy.wait_send()
 
     def drain(k):
-        for dx in (1, 2, 3):
+        for dx in (1, 3):
             wait_bytes(sep.at[k, x], b_ssem.at[k, dx - 1])
+            wait_bytes(sep.at[k, x, pl.ds(0, 128)], h_ssem.at[k, dx // 2])
         for f in range(4):
             wait_bytes(sep.at[k, f], f_ssem.at[k, f])
 
@@ -538,20 +578,19 @@
             V((8, 128), I32), V((8, 128), I32), V((1024, 128), F32), V((256, 1024), BF16),
             V((2, 128, 512), F32), V((3, 2, 1024, 128), F32),
             V((2, 256, 1024), F32), V((3, 2, 128, 1024), F32), V((128, 128), F32),
-            V((128, 1024), BF16), V((128, 1024), BF16),
+            V((256, 1024), BF16),
             V((3, 1024, 256), BF16), V((3, 1024, 256), BF16),
-            V((256, 2048), BF16), V((256, 2048), BF16),
-            V((3, 4, 128, 512), BF16), V((3, 4, 128, 512), BF16),
+            V((4, 512, 512), BF16), V((3, 4, 256, 512), BF16),
             V((2, 4, 2, 128, 128), F32), V((2, 32, 32, 128), F32),
             V((16, 1, 128), F32), V((2, 32, 1, 128), F32),
-            V((128, 512), F32), V((4, 32, 512), F32), V((128, 512), F32),
+            V((128, 512), F32), V((2, 4, 16, 512), F32), V((128, 512), F32),
             V((3, 512, 128), F32), V((3, 512, 128), F32), V((3, 512, 128), F32),
             V((4, 128, 128), F32), V((8, 64, 128), F32), V((16, 32, 128), F32),
             V((128, 128), F32), V((64, 128), F32), V((32, 128), F32),
             V((1024, 128), F32), V((3, 4, 256, 128), F32), V((128, 128), F32), V((128, 128), F32),
-            DMA((8,)), DMA((2,)), DMA((2, 4)), DMA((2,)), DMA((2, 4)), DMA, DMA, DMA((3,)), DMA((3,)),
-            DMA((3,)), DMA((3,)), DMA((3,)), DMA((3,)), DMA((3, 4)), DMA,
-            DMA((3,)), DMA((3, 3)), DMA((3, 4)), DMA((3, 4)),
+            DMA((8,)), DMA((2,)), DMA((2, 4)), DMA((2,)), DMA((2, 4)), DMA((2,)), DMA((2,)), DMA((2, 3)), DMA((2, 3)),
+            DMA((3,)), DMA((3,)), DMA((3,)), DMA((3,)), DMA((3, 4)), DMA((4,)),
+            DMA((3,)), DMA((3, 3)), DMA((3, 2)), DMA((3, 4)), DMA((3, 4)),
         ],
         compiler_params=pltpu.CompilerParams(
             collective_id=0, has_side_effects=True, vmem_limit_bytes=62 * 1024 * 1024

time: 76.1 us -> 75.3 us (0.989)
  Pallas kernels: 74.8 us -> 74 us
    pallas_call x1, Pallas kernels: 74.8 us -> 74 us  [local(): pl.pallas_call(kernel, out_shape=jax.ShapeDtypeStruct((1, 128), F32), in_...]
where the time goes in v4:
time: 75.3 us; the launch traced here: 75.2 us
  Pallas kernels  74 us (98%)
  local copies, waits for them, and re-layouts  1.19 us (2%)
    pallas_call x1, Pallas kernels, local(): pl.pallas_call(kernel, out_shape=jax.ShapeDtypeStruct((1, 128), F32), in_...  74 us

profile of v4, /device:TPU:1, one launch (start us, length us, event | category | flops | bytes accessed | tf_op | source)
XLA Modules:
  0.0 75.2 jit_solution(503767050331520028)
XLA Ops:
  0.0 74.0 %adjoint_gradient.1 = f32[1,128]{1,0:T(1,128)} custom-call(f32[1024,128]{1,0:T(8,128)} %resid.1, s32[8,128]{1,0:T(8,128)} %bitcast.11, s32[8,128]{1,0:T(8,128)} %bitcast.12, f32[2,128,512]{2,1,0:T(8,128)} %bitcast.10, f32[3,2,1024,128]{3,2,1,0:T(8,128)} %bitcast.7, f32[2,256,1024]{2,1,0:T(8,128)} %bitcast.9, f32[3,2,128,1024]{3,2,1,0:T(8,128)} %bitcast.8, ...), custom_call_target="tpu_custom_call" | custom-call | tf_op jit(solution)/shard_map/adjoint_gradient/pallas_call | solution.py:572
  74.0 1.2 %copy.10 = f32[128]{0:T(128)} copy(f32[128]{0:T(128)} %bitcast.13) | data formatting | bytes 1024

commit v5 on v4

--- a/solution.py
+++ b/solution.py
@@ -354,18 +354,18 @@
                     ).start()
         box[me] = t_sum[k, pl.ds(pl.multiple_of(me * rows, rows), rows)]
 
+    give(2)
+    t_sum[2] = term(2, ours)
     give(0)
+    scatter(2)
     t_sum[0] = term(0, ours)
-    give(2)
+    give(1)
     scatter(0)
-    t_sum[2] = term(2, ours)
-    give(1)
-    scatter(2)
     t_sum[1] = term(1, ours)
     scatter(1)
 
     targets = (leaf - c, base4 + 1, base8 + 3)
-    for k in (0, 2, 1):
+    for k in (2, 0, 1):
         box, total, span, rows, zk = stages[k]
         wait_bytes(box.at[pl.ds(0, 4 * span - 1)], rs_rsem.at[k])
         value = box[0]

time: 75.3 us -> 75.1 us (level)
  no operation moved by 1% of the time
where the time goes in v5:
time: 75.1 us; the launch traced here: 75 us
  Pallas kernels  73.8 us (98%)
  local copies, waits for them, and re-layouts  1.19 us (2%)
    pallas_call x1, Pallas kernels, local(): pl.pallas_call(kernel, out_shape=jax.ShapeDtypeStruct((1, 128), F32), in_...  73.8 us

profile of v5, /device:TPU:1, one launch (start us, length us, event | category | flops | bytes accessed | tf_op | source)
XLA Modules:
  0.0 75.0 jit_solution(2595245252802701414)
XLA Ops:
  0.0 73.8 %adjoint_gradient.1 = f32[1,128]{1,0:T(1,128)} custom-call(f32[1024,128]{1,0:T(8,128)} %resid.1, s32[8,128]{1,0:T(8,128)} %bitcast.11, s32[8,128]{1,0:T(8,128)} %bitcast.12, f32[2,128,512]{2,1,0:T(8,128)} %bitcast.10, f32[3,2,1024,128]{3,2,1,0:T(8,128)} %bitcast.7, f32[2,256,1024]{2,1,0:T(8,128)} %bitcast.9, f32[3,2,128,1024]{3,2,1,0:T(8,128)} %bitcast.8, ...), custom_call_target="tpu_custom_call" | custom-call | tf_op jit(solution)/shard_map/adjoint_gradient/pallas_call | solution.py:572
  73.8 1.2 %copy.10 = f32[128]{0:T(128)} copy(f32[128]{0:T(128)} %bitcast.13) | data formatting | bytes 1024
